TPU v7x, 32 devices: a whole 2x2x4 slice. The times are simulated.
32 devices in a mesh: col: 4 (over x, core), mem: 8 (over z, y).
Axes of the slice: x: 2, y: 2, z: 4, core: 2. Of those that a mesh axis runs over, the one named last changes fastest.
Arguments:
- members: bfloat16 [8, 128, 4096], P('mem', 'col'), may hold values from -15 to 15
- control: bfloat16 [128, 4096], P(None, 'col'), may hold values from -6 to 6
- vertical: bfloat16 [128, 128], replicated, may hold values from -0.5 to 0.5
- blocks: bfloat16 [32, 8, 128, 128], P('col'), may hold values from -0.1875 to 0.1875
- neighbours: int32 [32, 8], P('col'), may hold values from 0 to 31, as said below
- counts: int32 [32], P('col'), may hold values from 4 to 8, as said below
Outputs:
- increment: float32 [128, 4096], P('mem', 'col')
Inputs may be any that keep to these rules, and one draw needn't show every extreme that they name: neighbours[p, k] = (p + o) mod 32 with offsets o distinct within a row and -4 <= o <= 4. Entries of neighbours at k >= counts[p] are not used.
All inputs are finite; a program needn't handle non-finite values.
Results may differ from a plain program's by a relative error of at most 0.0041.
Values may be sent and summed in bfloat16 or wider, within the bound.
A program may use at most 64 MiB of HBM per device.

v0:
```python
import jax
import jax.numpy as jnp
from jax import lax
from jax.sharding import PartitionSpec as P

PATCH = 128
REACH = 4


def padded(cells, sides, width):
    for axis, dim in sides:
        count = lax.axis_size(axis)
        head = lax.slice_in_dim(cells, 0, width, axis=dim)
        tail = lax.slice_in_dim(cells, cells.shape[dim] - width, cells.shape[dim], axis=dim)
        cells = jnp.concatenate(
            [
                lax.ppermute(tail, axis, [(i, (i + 1) % count) for i in range(count)]),
                cells,
                lax.ppermute(head, axis, [((i + 1) % count, i) for i in range(count)]),
            ],
            axis=dim,
        )
    return cells


def per_device(members, control, vertical, blocks, neighbours, counts):
    control_wide = control.astype(jnp.float32)
    slab = lax.all_to_all(members, "col", split_axis=2, concat_axis=1, tiled=True)
    weighted = (slab.astype(jnp.float32) * control_wide[None]).astype(jnp.bfloat16)
    lifted = jnp.einsum("ab,kbc->kac", vertical, weighted, preferred_element_type=jnp.float32)
    local_members, lifted = (slab, lifted.astype(jnp.bfloat16))
    extended = padded(lifted, (("col", 2),), REACH * PATCH)
    count_members = extended.shape[0]
    count_levels = extended.shape[1]
    width = PATCH
    local_patches = neighbours.shape[0]
    grid_patches = extended.shape[2] // width
    patch_major = jnp.transpose(
        extended.reshape(count_members * count_levels, grid_patches, width), (1, 0, 2)
    )
    total_patches = local_patches * lax.axis_size("col")
    first_patch = lax.axis_index("col") * local_patches
    own_patches = first_patch + jnp.arange(local_patches, dtype=jnp.int32)
    shifted = jnp.remainder(neighbours - own_patches[:, None] + REACH, total_patches)
    positions = shifted + jnp.arange(local_patches, dtype=jnp.int32)[:, None]
    in_use = (jnp.arange(neighbours.shape[1])[None, :] < counts[:, None]).astype(jnp.float32)
    spread = jnp.zeros((local_patches, count_members * count_levels, width), jnp.float32)
    for k in range(neighbours.shape[1]):
        picked = jnp.take(patch_major, positions[:, k], axis=0)
        product = jnp.einsum(
            "prc,pdc->prd", picked, blocks[:, k], preferred_element_type=jnp.float32
        )
        spread = spread + in_use[:, k][:, None, None] * product
    spread_back = jnp.transpose(
        spread.reshape(local_patches, count_members, count_levels, width), (1, 2, 0, 3)
    )
    modulated = local_members.astype(jnp.float32) * spread_back.reshape(
        count_members, count_levels, local_patches * width
    )
    member_term = jnp.sum(modulated, axis=0)
    summed = lax.psum_scatter(member_term, "mem", scatter_dimension=0, tiled=True)
    member_total = count_members * lax.axis_size("mem")
    return summed / jnp.float32(member_total - 1)


def solution(mesh):
    placed = (
        P("mem", "col", None),
        P(None, "col"),
        P(),
        P("col", None, None, None),
        P("col", None),
        P("col"),
    )
    return jax.shard_map(
        per_device, mesh=mesh, in_specs=placed, out_specs=P("mem", "col"), check_vma=False
    )
```

profile of v0, /device:TPU:0, one launch (start us, length us, event | category | flops | bytes accessed | tf_op | source)
XLA Modules:
  0.0 146.2 jit_solution(15414524195864892015)
XLA Ops:
  6.5 4.5 %copy.28 = bf16[1,32,4096]{1,0,2:T(2,128)(2,1)S(1)} copy(bf16[1,32,4096]{2,1,0:T(8,128)(2,1)} %param.8) | data formatting | bytes 524288 | tf_op args[0]
  11.0 0.5 broadcast.176
  11.6 22.4 %reduce.16 = bf16[4096,32]{1,0:T(8,128)(2,1)S(1)} reduce(bf16[4096,1,32]{2,1,0:T(2,128)(2,1)S(1)} %bitcast.89, bf16[]{:T(256)} %broadcast.176), dimensions={1}, to_apply=%bitcast.75.reduce_sub_computation | reduce | bytes 524290
  34.0 1.7 %reshape.147 = bf16[4,2,16384]{2,1,0:T(2,128)(2,1)} reshape(bf16[4096,32]{1,0:T(8,128)(2,1)S(1)} %reduce.16) | data formatting | bytes 524288
  35.7 4.2 %all-to-all-start = ((bf16[4,2,16384]{2,1,0:T(2,128)(2,1)}), bf16[4,2,16384]{2,1,0:T(2,128)(2,1)S(1)}, u32[]{:S(2)}, u32[]{:S(2)}) async-start(bf16[4,2,16384]{2,1,0:T(2,128)(2,1)} %reshape.147), calls=%async_computation | async-start | bytes 524288 | tf_op jit(solution)/shard_map/all_to_all | solution.py:28
  40.5 5.4 %all-to-all-done = bf16[4,2,16384]{2,1,0:T(2,128)(2,1)S(1)} async-done(((bf16[4,2,16384]{2,1,0:T(2,128)(2,1)}), bf16[4,2,16384]{2,1,0:T(2,128)(2,1)S(1)}, u32[]{:S(2)}, u32[]{:S(2)}) %all-to-all-start) | async-done | bytes 262176 | tf_op jit(solution)/shard_map/all_to_all | solution.py:28
  45.9 2.4 %reshape.148 = bf16[4096,1,32]{2,1,0:T(2,128)(2,1)} reshape(bf16[4,2,16384]{2,1,0:T(2,128)(2,1)S(1)} %all-to-all-done) | data formatting | bytes 524288
  48.3 3.8 %bitcast_convert_fusion = f32[1,32,4096]{1,0,2:T(1,128)S(1)} fusion(bf16[4096,1,32]{2,1,0:T(2,128)(2,1)} %reshape.148), kind=kLoop, calls=%fused_computation.127 | loop fusion | flops 131072 | bytes 786432 | tf_op jit(solution)/shard_map/convert_element_type | solution.py:57
  52.1 0.6 copy.29
  52.7 0.4 copy-done.8
  53.5 0.5 collective-permute-start
  54.0 2.8 %collective-permute-done.1 = bf16[1,128,512]{1,2,0:T(8,128)(2,1)S(1)} collective-permute-done((bf16[1,128,512]{1,2,0:T(8,128)(2,1)S(1)}, bf16[1,128,512]{1,2,0:T(8,128)(2,1)S(1)}, u32[]{:S(2)}, u32[]{:S(2)}) %collective-permute-start.1) | collective-permute-done | bytes 131104 | tf_op jit(solution)/shard_map/ppermute | solution.py:19
  56.8 2.1 %collective-permute-done = bf16[1,128,512]{1,2,0:T(8,128)(2,1)S(1)} collective-permute-done((bf16[1,128,512]{1,2,0:T(8,128)(2,1)S(1)}, bf16[1,128,512]{1,2,0:T(8,128)(2,1)S(1)}, u32[]{:S(2)}, u32[]{:S(2)}) %collective-permute-start) | collective-permute-done | bytes 131104 | tf_op jit(solution)/shard_map/ppermute | solution.py:17
  59.3 0.6 gather_fusion
  59.9 1.3 gather_fusion.1
  61.2 1.3 gather_fusion.2
  62.4 1.3 gather_fusion.3
  63.7 1.3 gather_fusion.4
  65.0 1.3 gather_fusion.5
  66.3 1.3 gather_fusion.6
  67.6 1.3 gather_fusion.7
  68.9 0.4 convolution_multiply_fusion.7
  69.3 1.4 fusion.6
  70.7 0.4 fusion.5
  71.1 0.4 fusion.4
  71.5 0.4 fusion.3
  71.9 0.4 fusion.2
  72.3 0.4 fusion.1
  72.7 0.4 fusion
  73.2 0.9 bitcast_multiply_fusion
  74.1 63.8 %reduce-scatter.2.cloned.1.call-done = f32[16,1024]{1,0:T(8,128)} async-done(((f32[128,1024]{1,0:T(8,128)}), f32[16,1024]{1,0:T(8,128)}) %reduce-scatter.2.cloned.1.call-update) | async-done | bytes 65552 | tf_op jit(solution)/shard_map/reduce_scatter | solution.py:61
  137.9 1.5 %broadcast_multiply_fusion = f32[16,1024]{1,0:T(8,128)} fusion(f32[16,1024]{1,0:T(8,128)} %reduce-scatter.2.cloned.1.call-done), kind=kLoop, calls=%fused_computation.69 | loop fusion | flops 16384 | bytes 131072 | tf_op jit(solution)/shard_map/div | solution.py:63
  (51 shorter events, 1.5 us)
Async XLA Ops:
  6.5 46.6 %copy-start = (bf16[128,128]{1,0:T(8,128)(2,1)S(1)}, bf16[128,128]{1,0:T(8,128)(2,1)}, u32[]{:S(2)}) copy-start(bf16[128,128]{1,0:T(8,128)(2,1)} %param.10) | copy-start | bytes 98308
  11.6 28.3 %copy-start.9 = (s32[8,8]{1,0:T(8,128)S(1)}, s32[8,8]{1,0:T(8,128)}, u32[]{:S(2)}) copy-start(s32[8,8]{1,0:T(8,128)} %param.12) | copy-start | bytes 772
  11.6 28.8 %copy-start.10 = (s32[8]{0:T(128)S(1)}, s32[8]{0:T(128)}, u32[]{:S(2)}) copy-start(s32[8]{0:T(128)} %param.13) | copy-start | bytes 100
  35.7 10.2 %all-to-all-start = ((bf16[4,2,16384]{2,1,0:T(2,128)(2,1)}), bf16[4,2,16384]{2,1,0:T(2,128)(2,1)S(1)}, u32[]{:S(2)}, u32[]{:S(2)}) async-start(bf16[4,2,16384]{2,1,0:T(2,128)(2,1)} %reshape.147), calls=%async_computation | async-start | bytes 524288 | tf_op jit(solution)/shard_map/all_to_all | solution.py:28
  39.9 98.0 %reduce-scatter.2.cloned.1.call-start = ((), (), s32[]{:S(2)}) async-start(), calls=%async_computation.2 | async-start | bytes 589824 | tf_op jit(solution)/shard_map/reduce_scatter | solution.py:61
  52.1 1.0 copy-start.8
  53.4 3.4 %collective-permute-start.1 = (bf16[1,128,512]{1,2,0:T(8,128)(2,1)S(1)}, bf16[1,128,512]{1,2,0:T(8,128)(2,1)S(1)}, u32[]{:S(2)}, u32[]{:S(2)}) collective-permute-start(bf16[1,128,512]{1,2,0:T(8,128)(2,1)S(1)} %get-tuple-element.15), channel_id=1, source_target_pairs={{8,0},{16,8},{24,16},{0,24},{9,1},{17,9},{25,17},{1,25},{10,2},{18... | collective-permute-start | bytes 393224 | tf_op jit(solution)/shard_map/ppermute | solution.py:19
  53.5 5.5 %collective-permute-start = (bf16[1,128,512]{1,2,0:T(8,128)(2,1)S(1)}, bf16[1,128,512]{1,2,0:T(8,128)(2,1)S(1)}, u32[]{:S(2)}, u32[]{:S(2)}) collective-permute-start(bf16[1,128,512]{1,2,0:T(8,128)(2,1)S(1)} %get-tuple-element.14), channel_id=1, source_target_pairs={{0,8},{8,16},{16,24},{24,0},{1,9},{9,17},{17,25},{25,1},{2,10},{10... | collective-permute-start | bytes 393224 | tf_op jit(solution)/shard_map/ppermute | solution.py:17
  59.3 9.6 %copy-start.1 = (bf16[8,8,128,128]{3,2,1,0:T(8,128)(2,1)S(1)}, bf16[8,8,128,128]{3,2,1,0:T(8,128)(2,1)}, u32[]{:S(2)}) copy-start(bf16[8,8,128,128]{3,2,1,0:T(8,128)(2,1)} %param.11) | copy-start | bytes 6291460
  68.9 1.8 %copy-start.7 = (bf16[8,128,128]{2,1,0:T(8,128)(2,1)S(1)}, bf16[8,128,128]{2,1,0:T(8,128)(2,1)}, u32[]{:S(2)}) copy-start(bf16[8,128,128]{2,1,0:T(8,128)(2,1)} %gather_fusion.2) | copy-start | bytes 786436
  68.9 2.2 %copy-start.6 = (bf16[8,128,128]{2,1,0:T(8,128)(2,1)S(1)}, bf16[8,128,128]{2,1,0:T(8,128)(2,1)}, u32[]{:S(2)}) copy-start(bf16[8,128,128]{2,1,0:T(8,128)(2,1)} %gather_fusion.3) | copy-start | bytes 786436
  69.3 2.2 %copy-start.5 = (bf16[8,128,128]{2,1,0:T(8,128)(2,1)S(1)}, bf16[8,128,128]{2,1,0:T(8,128)(2,1)}, u32[]{:S(2)}) copy-start(bf16[8,128,128]{2,1,0:T(8,128)(2,1)} %gather_fusion.4) | copy-start | bytes 786436
  70.7 1.2 copy-start.4
  71.1 1.2 copy-start.3
  71.5 1.2 copy-start.2
Sparse Core Ops, SparseCore 0:
  74.2 63.6 reduce-scatter.1
where the time goes:
time: 147 us; the launch traced here: 146 us
  waiting for transfers between devices  74.2 us (50%)
  other arithmetic  28.8 us (20%)
  local copies, waits for them, and re-layouts  20.4 us (14%)
  between operations  13.8 us (9%)
  starting transfers between devices  4.76 us (3%)
  matrix products  4.26 us (3%)
    reduce_scatter x1, waiting for transfers between devices, per_device(): lax.psum_scatter(member_term, 'mem', scatter_dimension=0, tiled=True)  63.8 us
    unnamed x1, other arithmetic  22.4 us
    gather x8, local copies, waits for them, and re-layouts, per_device(): picked = jnp.take(patch_major, positions[:, k], axis=0)  9.58 us
    unnamed x26, local copies, waits for them, and re-layouts  9.47 us
    all_to_all x1, waiting for transfers between devices, per_device(): lax.all_to_all(members, 'col', split_axis=2, concat_axis=1, tiled=True)  5.4 us
    all_to_all x1, starting transfers between devices, per_device(): lax.all_to_all(members, 'col', split_axis=2, concat_axis=1, tiled=True)  4.21 us
    dot_general x8, matrix products, per_device(): jnp.einsum('prc,pdc->prd', picked, blocks[:, k], preferred_element_type=j...  4 us
    convert_element_type x1, other arithmetic, per_device(): local_members.astype(jnp.float32)  3.77 us
  transfers between devices with their start and end apart: 4, of which 4 were waited for; matrix products, arithmetic and copies ran while one was open for 0% of the time, Pallas kernels for 0%

commit v1 on v0

v1 whole, which is shorter than its diff:
```python
import functools

import jax
import jax.numpy as jnp
from jax import lax
from jax.experimental import pallas as pl
from jax.experimental.pallas import tpu as pltpu
from jax.sharding import PartitionSpec as P

PATCH = 128
REACH = 4
MESH = pl.DeviceIdType.MESH


def kernel(
    ncol, nmem, members, control, vertical, blocks, near_ids, counts, out_ref,
    held, ctl, vert, blk, fields, late, stage, landed,
    load_sem, slab_send, slab_recv, far_send, far_recv, near_send, near_recv, sum_send, sum_recv,
):
    me, mine = lax.axis_index("col"), lax.axis_index("mem")
    first = lax.rem(me, 2)
    second = 1 - first
    levels = vertical.shape[0]
    width = REACH * PATCH
    columns = 2 * width
    share = levels // nmem
    total = ncol * 2 * REACH
    slots = near_ids.shape[1]
    blank = 4 * REACH

    loads = [
        pltpu.make_async_copy(control, ctl, load_sem.at[0]),
        pltpu.make_async_copy(vertical, vert, load_sem.at[1]),
        pltpu.make_async_copy(blocks, blk, load_sem.at[2]),
    ]
    for load in loads:
        load.start()

    barrier = pltpu.get_barrier_semaphore()
    for s in range(1, ncol):
        pl.semaphore_signal(barrier, inc=1, device_id={"col": lax.rem(me + s, ncol)}, device_id_type=MESH)
    for s in range(1, nmem):
        pl.semaphore_signal(barrier, inc=1, device_id={"mem": lax.rem(mine + s, nmem)}, device_id_type=MESH)
    fields[blank] = jnp.zeros((levels, PATCH), fields.dtype)
    pl.semaphore_wait(barrier, ncol + nmem - 2)

    for turn in range(2):
        for s in range(ncol):
            to = lax.rem(me + s, ncol)
            half = lax.rem(to + turn, 2)
            start = pl.multiple_of(to * columns + half * width, width)
            source = members.at[0, :, pl.ds(start, width)]
            if s == 0:
                pltpu.make_async_copy(source, held.at[half, me], slab_recv.at[half]).start()
            else:
                pltpu.make_async_remote_copy(
                    src_ref=source, dst_ref=held.at[half, me],
                    send_sem=slab_send.at[turn], recv_sem=slab_recv.at[half],
                    device_id={"col": to}, device_id_type=MESH,
                ).start()

    def lift(half):
        pltpu.make_async_copy(held.at[half], held.at[half], slab_recv.at[half]).wait()
        slab = held[half].astype(jnp.float32).reshape(levels, width)
        scale = ctl[:, pl.ds(pl.multiple_of(half * width, width), width)].astype(jnp.float32)
        weighted = (slab * scale).astype(jnp.bfloat16)
        lifted = jnp.dot(vert[...], weighted, preferred_element_type=jnp.float32).astype(jnp.bfloat16)
        for q in range(REACH):
            fields[REACH + REACH * half + q] = lifted[:, q * PATCH : (q + 1) * PATCH]

    def spread_patch(half, q):
        patch = half * REACH + q
        own = me * (2 * REACH) + patch
        used = counts[patch]
        tiles = []
        for k in range(slots):
            offset = near_ids[patch, k] - own + REACH
            offset = jnp.where(offset < 0, offset + total, offset)
            offset = jnp.where(offset >= total, offset - total, offset)
            tiles.append(fields[jnp.where(k < used, offset + patch, blank)])
        weights = [blk[patch, k] for k in range(slots)]
        spread = lax.dot_general(
            jnp.concatenate(tiles, axis=1), jnp.concatenate(weights, axis=1),
            (((1,), (1,)), ((), ())), preferred_element_type=jnp.float32,
        )
        slab = held[half, :, :, pl.ds(pl.multiple_of(q * PATCH, PATCH), PATCH)]
        term = slab.astype(jnp.float32).reshape(levels, PATCH) * spread
        term = term.astype(jnp.bfloat16)
        group = half * 2 + q // 2
        place = pl.ds(pl.multiple_of((q % 2) * PATCH, PATCH), PATCH)
        for j in range(nmem):
            stage[group, j, :, place] = term[j * share : (j + 1) * share]

    def send_group(group):
        for s in range(1, nmem):
            to = lax.rem(mine + s, nmem)
            pltpu.make_async_remote_copy(
                src_ref=stage.at[group, to], dst_ref=landed.at[group, mine],
                send_sem=sum_send.at[group], recv_sem=sum_recv.at[group],
                device_id={"mem": to}, device_id_type=MESH,
            ).start()
        landed[group, mine] = stage[group, mine]

    def add_group(group):
        pieces = landed.at[group, pl.ds(0, nmem - 1)]
        pltpu.make_async_copy(pieces, pieces, sum_recv.at[group]).wait()
        summed = jnp.sum(landed[group].astype(jnp.float32), axis=0)
        place = pl.ds(pl.multiple_of(group * 2 * PATCH, 2 * PATCH), 2 * PATCH)
        out_ref[:, place] = summed / jnp.float32(nmem - 1)

    loads[0].wait()
    loads[1].wait()
    lift(first)
    far = []
    for s in range(REACH):
        q = s + first * (REACH - 1 - 2 * s)
        far.append(
            pltpu.make_async_remote_copy(
                src_ref=fields.at[REACH + REACH * first + q], dst_ref=late.at[q],
                send_sem=far_send.at[s], recv_sem=far_recv.at[s],
                device_id={"col": lax.rem(me + ncol + 2 * first - 1, ncol)}, device_id_type=MESH,
            )
        )
        far[-1].start()
    lift(second)
    near = pltpu.make_async_remote_copy(
        src_ref=fields.at[pl.ds(REACH + REACH * second, REACH)],
        dst_ref=fields.at[pl.ds(3 * REACH * first, REACH)],
        send_sem=near_send, recv_sem=near_recv,
        device_id={"col": lax.rem(me + ncol + 2 * second - 1, ncol)}, device_id_type=MESH,
    )
    near.start()
    loads[2].wait()
    near.wait_recv()

    for q in range(REACH):
        spread_patch(second, q)
        if q % 2 == 1:
            send_group(second * 2 + q // 2)

    for s in range(REACH):
        q = s + second * (REACH - 1 - 2 * s)
        far[s].wait_recv()
        fields[3 * REACH * first + q] = late[q]
        spread_patch(first, q)
        if s % 2 == 1:
            send_group(first * 2 + q // 2)

    add_group(second * 2)
    add_group(second * 2 + 1)
    add_group(first * 2 + second)
    add_group(first * 2 + first)

    for turn in range(2):
        pieces = held.at[turn, pl.ds(0, ncol - 1)]
        pltpu.make_async_copy(pieces, pieces, slab_send.at[turn]).wait()
    for copy in far:
        copy.wait_send()
    near.wait_send()
    for group in range(4):
        pieces = stage.at[group, pl.ds(0, nmem - 1)]
        pltpu.make_async_copy(pieces, pieces, sum_send.at[group]).wait()


def solution(mesh):
    ncol, nmem = mesh.shape["col"], mesh.shape["mem"]

    def per_device(members, control, vertical, blocks, neighbours, counts):
        levels, columns = control.shape
        patches, slots = neighbours.shape
        slab_rows = members.shape[1]
        assert members.shape[0] == 1 and patches == 2 * REACH and ncol % 2 == 0
        share = levels // nmem
        bf16 = jnp.bfloat16
        dma = pltpu.SemaphoreType.DMA
        anywhere = pl.BlockSpec(memory_space=pl.ANY)
        scalars = pl.BlockSpec(memory_space=pltpu.SMEM)
        return pl.pallas_call(
            functools.partial(kernel, ncol, nmem),
            out_shape=jax.ShapeDtypeStruct((share, columns), jnp.float32),
            in_specs=[anywhere] * 4 + [scalars] * 2,
            out_specs=pl.BlockSpec(memory_space=pltpu.VMEM),
            scratch_shapes=[
                pltpu.VMEM((2, ncol, slab_rows, columns // 2), bf16),
                pltpu.VMEM((levels, columns), bf16),
                pltpu.VMEM((levels, levels), bf16),
                pltpu.VMEM((patches, slots, PATCH, PATCH), bf16),
                pltpu.VMEM((4 * REACH + 1, levels, PATCH), bf16),
                pltpu.VMEM((REACH, levels, PATCH), bf16),
                pltpu.VMEM((4, nmem, share, 2 * PATCH), bf16),
                pltpu.VMEM((4, nmem, share, 2 * PATCH), bf16),
                dma((3,)), dma((2,)), dma((2,)), dma((REACH,)), dma((REACH,)), dma, dma, dma((4,)), dma((4,)),
            ],
            compiler_params=pltpu.CompilerParams(
                collective_id=0, has_side_effects=True, vmem_limit_bytes=48 * 1024 * 1024
            ),
            name="localized_covariance",
        )(members, control, vertical, blocks, neighbours, counts)

    placed = (
        P("mem", "col", None),
        P(None, "col"),
        P(),
        P("col", None, None, None),
        P("col", None),
        P("col"),
    )
    return jax.shard_map(
        per_device, mesh=mesh, in_specs=placed, out_specs=P("mem", "col"), check_vma=False
    )
```

time: 147 us -> 26.7 us (0.18)
  waiting for transfers between devices: 74.2 us -> 0 us
  other arithmetic: 28.8 us -> 0 us
  Pallas kernels: 0 us -> 20.1 us
  local copies, waits for them, and re-layouts: 20.4 us -> 6.22 us
  between operations: 13.8 us -> 0.02 us
  starting transfers between devices: 4.76 us -> 0 us
  matrix products: 4.26 us -> 0 us
    reduce_scatter x1 -> x0, waiting for transfers between devices: 63.8 us -> none  [per_device(): lax.psum_scatter(member_term, 'mem', scatter_dimension=0, tiled=True)]
    unnamed x1 -> x0, other arithmetic: 22.4 us -> none
    pallas_call x0 -> x1, Pallas kernels: none -> 20.1 us  [per_device(): pl.pallas_call(functools.partial(kernel, ncol, nmem), out_shape=jax.Shape...]
    gather x8 -> x0, local copies, waits for them, and re-layouts: 9.58 us -> none  [per_device(): picked = jnp.take(patch_major, positions[:, k], axis=0)]
    all_to_all x1 -> x0, waiting for transfers between devices: 5.4 us -> none  [per_device(): lax.all_to_all(members, 'col', split_axis=2, concat_axis=1, tiled=True)]
    ppermute x2 -> x0, waiting for transfers between devices: 4.98 us -> none  [the longest x1 2.85 us: padded(): lax.ppermute(head, axis, [((i + 1) % count, i) for i in range(count)])]
    dot_general x9 -> x0, matrix products: 4.26 us -> none  [the longest x8 4 us: per_device(): jnp.einsum('prc,pdc->prd', picked, blocks[:, k], preferred_element_type=j...]
    all_to_all x1 -> x0, starting transfers between devices: 4.21 us -> none  [per_device(): lax.all_to_all(members, 'col', split_axis=2, concat_axis=1, tiled=True)]
  transfers between devices with their start and end apart: 4 -> 0, of which waited for: 4 -> 0; matrix products, arithmetic and copies ran while one was open for 0% -> 0% of each run, Pallas kernels for 0% -> 0%
where the time goes in v1:
time: 26.7 us; the launch traced here: 26.4 us
  Pallas kernels  20.1 us (75%)
  local copies, waits for them, and re-layouts  6.22 us (23%)
    pallas_call x1, Pallas kernels, per_device(): pl.pallas_call(functools.partial(kernel, ncol, nmem), out_shape=jax.Shape...  20.1 us
    unnamed x13, local copies, waits for them, and re-layouts  6.22 us

profile of v1, /device:TPU:0, one launch (start us, length us, event | category | flops | bytes accessed | tf_op | source)
XLA Modules:
  0.0 26.4 jit_solution(6614300325862921089)
XLA Ops:
  0.0 0.0 copy-start
  0.0 1.6 %copy-done = bf16[8,8,128,128]{3,2,1,0:T(8,128)(2,1)S(1)} copy-done((bf16[8,8,128,128]{3,2,1,0:T(8,128)(2,1)S(1)}, bf16[8,8,128,128]{3,2,1,0:T(8,128)(2,1)}, u32[]{:S(2)}) %copy-start) | copy-done | bytes 2097176
  1.6 0.0 copy-start.1
  1.6 0.9 %copy-done.1 = bf16[1,32,4096]{2,1,0:T(8,128)(2,1)S(1)} copy-done((bf16[1,32,4096]{2,1,0:T(8,128)(2,1)S(1)}, bf16[1,32,4096]{2,1,0:T(8,128)(2,1)}, u32[]{:S(2)}) %copy-start.1) | copy-done | bytes 262168
  2.5 0.0 copy-start.2
  2.5 0.9 %copy-done.2 = bf16[128,1024]{1,0:T(8,128)(2,1)S(1)} copy-done((bf16[128,1024]{1,0:T(8,128)(2,1)S(1)}, bf16[128,1024]{1,0:T(8,128)(2,1)}, u32[]{:S(2)}) %copy-start.2) | copy-done | bytes 262168
  3.5 0.0 copy-start.3
  3.5 0.8 %copy-done.3 = bf16[128,128]{1,0:T(8,128)(2,1)S(1)} copy-done((bf16[128,128]{1,0:T(8,128)(2,1)S(1)}, bf16[128,128]{1,0:T(8,128)(2,1)}, u32[]{:S(2)}) %copy-start.3) | copy-done | bytes 32792
  4.3 0.0 copy-start.4
  4.3 0.7 %copy-done.4 = s32[8,8]{1,0:T(8,128)S(1)} copy-done((s32[8,8]{1,0:T(8,128)S(1)}, s32[8,8]{1,0:T(8,128)}, u32[]{:S(2)}) %copy-start.4) | copy-done | bytes 280
  4.9 0.0 copy-start.5
  4.9 0.7 %copy-done.5 = s32[8]{0:T(128)S(1)} copy-done((s32[8]{0:T(128)S(1)}, s32[8]{0:T(128)}, u32[]{:S(2)}) %copy-start.5) | copy-done | bytes 56
  5.6 20.1 %localized_covariance.1 = f32[16,1024]{1,0:T(8,128)S(1)} custom-call(bf16[1,32,4096]{2,1,0:T(8,128)(2,1)S(1)} %copy-done.1, bf16[128,1024]{1,0:T(8,128)(2,1)S(1)} %copy-done.2, bf16[128,128]{1,0:T(8,128)(2,1)S(1)} %copy-done.3, bf16[8,8,128,128]{3,2,1,0:T(8,128)(2,1)S(1)} %copy-done, s32[8,8]{1,0:T(8,128)S(1)} %copy-done.4, s32[8]{0:T(128)S(1)} %copy-done.5), custom_call_target="tpu_custom_call" | custom-call | tf_op jit(solution)/shard_map/localized_covariance/pallas_call | solution.py:178
  25.7 0.6 %copy.8 = f32[16,1024]{1,0:T(8,128)} copy(f32[16,1024]{1,0:T(8,128)S(1)} %localized_covariance.1) | data formatting | bytes 131072
Async XLA Ops:
  0.0 1.6 %copy-start = (bf16[8,8,128,128]{3,2,1,0:T(8,128)(2,1)S(1)}, bf16[8,8,128,128]{3,2,1,0:T(8,128)(2,1)}, u32[]{:S(2)}) copy-start(bf16[8,8,128,128]{3,2,1,0:T(8,128)(2,1)} %blocks.1) | copy-start | bytes 6291460
  1.6 0.9 %copy-start.1 = (bf16[1,32,4096]{2,1,0:T(8,128)(2,1)S(1)}, bf16[1,32,4096]{2,1,0:T(8,128)(2,1)}, u32[]{:S(2)}) copy-start(bf16[1,32,4096]{2,1,0:T(8,128)(2,1)} %members.1) | copy-start | bytes 786436
  2.5 0.9 %copy-start.2 = (bf16[128,1024]{1,0:T(8,128)(2,1)S(1)}, bf16[128,1024]{1,0:T(8,128)(2,1)}, u32[]{:S(2)}) copy-start(bf16[128,1024]{1,0:T(8,128)(2,1)} %control.1) | copy-start | bytes 786436
  3.5 0.8 %copy-start.3 = (bf16[128,128]{1,0:T(8,128)(2,1)S(1)}, bf16[128,128]{1,0:T(8,128)(2,1)}, u32[]{:S(2)}) copy-start(bf16[128,128]{1,0:T(8,128)(2,1)} %vertical.1) | copy-start | bytes 98308
  4.3 0.7 %copy-start.4 = (s32[8,8]{1,0:T(8,128)S(1)}, s32[8,8]{1,0:T(8,128)}, u32[]{:S(2)}) copy-start(s32[8,8]{1,0:T(8,128)} %near_ids.1) | copy-start | bytes 772
  4.9 0.7 %copy-start.5 = (s32[8]{0:T(128)S(1)}, s32[8]{0:T(128)}, u32[]{:S(2)}) copy-start(s32[8]{0:T(128)} %counts.1) | copy-start | bytes 100

commit v2 on v1

--- a/solution.py
+++ b/solution.py
@@ -13,8 +13,8 @@
 
 
 def kernel(
-    ncol, nmem, members, control, vertical, blocks, near_ids, counts, out_ref,
-    held, ctl, vert, blk, fields, late, stage, landed,
+    ncol, nmem, members, control, vertical, blocks, neighbours, counts_in, out_ref,
+    near_ids, counts, held, ctl, vert, blk, fields, late, stage, landed,
     load_sem, slab_send, slab_recv, far_send, far_recv, near_send, near_recv, sum_send, sum_recv,
 ):
     me, mine = lax.axis_index("col"), lax.axis_index("mem")
@@ -32,6 +32,8 @@
         pltpu.make_async_copy(control, ctl, load_sem.at[0]),
         pltpu.make_async_copy(vertical, vert, load_sem.at[1]),
         pltpu.make_async_copy(blocks, blk, load_sem.at[2]),
+        pltpu.make_async_copy(neighbours, near_ids, load_sem.at[3]),
+        pltpu.make_async_copy(counts_in, counts, load_sem.at[4]),
     ]
     for load in loads:
         load.start()
@@ -130,7 +132,8 @@
         device_id={"col": lax.rem(me + ncol + 2 * second - 1, ncol)}, device_id_type=MESH,
     )
     near.start()
-    loads[2].wait()
+    for load in loads[2:]:
+        load.wait()
     near.wait_recv()
 
     for q in range(REACH):
@@ -173,14 +176,15 @@
         share = levels // nmem
         bf16 = jnp.bfloat16
         dma = pltpu.SemaphoreType.DMA
-        anywhere = pl.BlockSpec(memory_space=pl.ANY)
-        scalars = pl.BlockSpec(memory_space=pltpu.SMEM)
+        in_hbm = pl.BlockSpec(memory_space=pltpu.HBM)
         return pl.pallas_call(
             functools.partial(kernel, ncol, nmem),
             out_shape=jax.ShapeDtypeStruct((share, columns), jnp.float32),
-            in_specs=[anywhere] * 4 + [scalars] * 2,
+            in_specs=[in_hbm] * 6,
             out_specs=pl.BlockSpec(memory_space=pltpu.VMEM),
             scratch_shapes=[
+                pltpu.SMEM((patches, slots), jnp.int32),
+                pltpu.SMEM((patches,), jnp.int32),
                 pltpu.VMEM((2, ncol, slab_rows, columns // 2), bf16),
                 pltpu.VMEM((levels, columns), bf16),
                 pltpu.VMEM((levels, levels), bf16),
@@ -189,10 +193,10 @@
                 pltpu.VMEM((REACH, levels, PATCH), bf16),
                 pltpu.VMEM((4, nmem, share, 2 * PATCH), bf16),
                 pltpu.VMEM((4, nmem, share, 2 * PATCH), bf16),
-                dma((3,)), dma((2,)), dma((2,)), dma((REACH,)), dma((REACH,)), dma, dma, dma((4,)), dma((4,)),
+                dma((5,)), dma((2,)), dma((2,)), dma((REACH,)), dma((REACH,)), dma, dma, dma((4,)), dma((4,)),
             ],
             compiler_params=pltpu.CompilerParams(
-                collective_id=0, has_side_effects=True, vmem_limit_bytes=48 * 1024 * 1024
+                collective_id=0, has_side_effects=True, vmem_limit_bytes=60 * 1024 * 1024
             ),
             name="localized_covariance",
         )(members, control, vertical, blocks, neighbours, counts)

time: 26.7 us -> 21.7 us (0.81)
  local copies, waits for them, and re-layouts: 6.22 us -> 1.47 us
    unnamed x13 -> x1, local copies, waits for them, and re-layouts: 6.22 us -> 1.47 us
where the time goes in v2:
time: 21.7 us; the launch traced here: 21.6 us
  Pallas kernels  20.1 us (93%)
  local copies, waits for them, and re-layouts  1.47 us (7%)
    pallas_call x1, Pallas kernels, per_device(): pl.pallas_call(functools.partial(kernel, ncol, nmem), out_shape=jax.Shape...  20.1 us
    unnamed x1, local copies, waits for them, and re-layouts  1.47 us

profile of v2, /device:TPU:0, one launch (start us, length us, event | category | flops | bytes accessed | tf_op | source)
XLA Modules:
  0.0 21.6 jit_solution(8439888498740651522)
XLA Ops:
  0.0 20.1 %localized_covariance.1 = f32[16,1024]{1,0:T(8,128)} custom-call(bf16[1,32,4096]{2,1,0:T(8,128)(2,1)} %members.1, bf16[128,1024]{1,0:T(8,128)(2,1)} %control.1, bf16[128,128]{1,0:T(8,128)(2,1)} %vertical.1, bf16[8,8,128,128]{3,2,1,0:T(8,128)(2,1)} %blocks.1, s32[8,8]{1,0:T(8,128)} %neighbours.1, s32[8]{0:T(128)} %counts_in.1), custom_call_target="tpu_custom_call" | custom-call | tf_op jit(solution)/shard_map/localized_covariance/pallas_call | solution.py:180
  20.1 1.5 %copy.8 = f32[16,1024]{1,0:T(8,128)} copy(f32[16,1024]{1,0:T(8,128)} %localized_covariance.1) | data formatting | bytes 131072

commit v3 on v2

--- a/solution.py
+++ b/solution.py
@@ -15,7 +15,7 @@
 def kernel(
     ncol, nmem, members, control, vertical, blocks, neighbours, counts_in, out_ref,
     near_ids, counts, held, ctl, vert, blk, fields, late, stage, landed,
-    load_sem, slab_send, slab_recv, far_send, far_recv, near_send, near_recv, sum_send, sum_recv,
+    load_sem, slab_send, slab_recv, far_send, far_recv, near_send, near_recv, sum_send, sum_recv, joined, ready,
 ):
     me, mine = lax.axis_index("col"), lax.axis_index("mem")
     first = lax.rem(me, 2)
@@ -39,12 +39,26 @@
         load.start()
 
     barrier = pltpu.get_barrier_semaphore()
+    leads = me == 0
     for s in range(1, ncol):
-        pl.semaphore_signal(barrier, inc=1, device_id={"col": lax.rem(me + s, ncol)}, device_id_type=MESH)
-    for s in range(1, nmem):
-        pl.semaphore_signal(barrier, inc=1, device_id={"mem": lax.rem(mine + s, nmem)}, device_id_type=MESH)
+        to = lax.rem(me + s, ncol)
+
+        @pl.when(to != 0)
+        def _():
+            pl.semaphore_signal(barrier, inc=1, device_id={"col": to}, device_id_type=MESH)
+
     fields[blank] = jnp.zeros((levels, PATCH), fields.dtype)
-    pl.semaphore_wait(barrier, ncol + nmem - 2)
+
+    @pl.when(leads)
+    def _():
+        pl.semaphore_wait(joined, ncol - 1)
+        for s in range(1, nmem):
+            pl.semaphore_signal(barrier, inc=1, device_id={"mem": lax.rem(mine + s, nmem)}, device_id_type=MESH)
+
+    @pl.when(jnp.logical_not(leads))
+    def _():
+        pl.semaphore_wait(barrier, ncol - 1)
+        pl.semaphore_signal(joined, inc=1, device_id={"col": 0}, device_id_type=MESH)
 
     for turn in range(2):
         for s in range(ncol):
@@ -132,9 +146,20 @@
         device_id={"col": lax.rem(me + ncol + 2 * second - 1, ncol)}, device_id_type=MESH,
     )
     near.start()
+
+    @pl.when(leads)
+    def _():
+        pl.semaphore_wait(barrier, nmem - 1)
+        for s in range(1, ncol):
+            pl.semaphore_signal(ready, inc=1, device_id={"col": lax.rem(me + s, ncol)}, device_id_type=MESH)
+
     for load in loads[2:]:
         load.wait()
     near.wait_recv()
+
+    @pl.when(jnp.logical_not(leads))
+    def _():
+        pl.semaphore_wait(ready, 1)
 
     for q in range(REACH):
         spread_patch(second, q)
@@ -194,6 +219,7 @@
                 pltpu.VMEM((4, nmem, share, 2 * PATCH), bf16),
                 pltpu.VMEM((4, nmem, share, 2 * PATCH), bf16),
                 dma((5,)), dma((2,)), dma((2,)), dma((REACH,)), dma((REACH,)), dma, dma, dma((4,)), dma((4,)),
+                pltpu.SemaphoreType.REGULAR, pltpu.SemaphoreType.REGULAR,
             ],
             compiler_params=pltpu.CompilerParams(
                 collective_id=0, has_side_effects=True, vmem_limit_bytes=60 * 1024 * 1024

time: 21.7 us -> 20.9 us (0.963)
  Pallas kernels: 20.1 us -> 19.3 us
    pallas_call x1, Pallas kernels: 20.1 us -> 19.3 us  [per_device(): pl.pallas_call(functools.partial(kernel, ncol, nmem), out_shape=jax.Shape...]
where the time goes in v3:
time: 20.9 us; the launch traced here: 20.8 us
  Pallas kernels  19.3 us (92%)
  local copies, waits for them, and re-layouts  1.47 us (7%)
    pallas_call x1, Pallas kernels, per_device(): pl.pallas_call(functools.partial(kernel, ncol, nmem), out_shape=jax.Shape...  19.3 us
    unnamed x1, local copies, waits for them, and re-layouts  1.47 us

profile of v3, /device:TPU:0, one launch (start us, length us, event | category | flops | bytes accessed | tf_op | source)
XLA Modules:
  0.0 20.8 jit_solution(4896649057759167283)
XLA Ops:
  0.0 19.3 %localized_covariance.1 = f32[16,1024]{1,0:T(8,128)} custom-call(bf16[1,32,4096]{2,1,0:T(8,128)(2,1)} %members.1, bf16[128,1024]{1,0:T(8,128)(2,1)} %control.1, bf16[128,128]{1,0:T(8,128)(2,1)} %vertical.1, bf16[8,8,128,128]{3,2,1,0:T(8,128)(2,1)} %blocks.1, s32[8,8]{1,0:T(8,128)} %neighbours.1, s32[8]{0:T(128)} %counts_in.1), custom_call_target="tpu_custom_call" | custom-call | tf_op jit(solution)/shard_map/localized_covariance/pallas_call | solution.py:205
  19.3 1.5 %copy.8 = f32[16,1024]{1,0:T(8,128)} copy(f32[16,1024]{1,0:T(8,128)} %localized_covariance.1) | data formatting | bytes 131072

commit v4 on v3

--- a/solution.py
+++ b/solution.py
@@ -102,8 +102,8 @@
         slab = held[half, :, :, pl.ds(pl.multiple_of(q * PATCH, PATCH), PATCH)]
         term = slab.astype(jnp.float32).reshape(levels, PATCH) * spread
         term = term.astype(jnp.bfloat16)
-        group = half * 2 + q // 2
-        place = pl.ds(pl.multiple_of((q % 2) * PATCH, PATCH), PATCH)
+        group = half
+        place = pl.ds(pl.multiple_of(q * PATCH, PATCH), PATCH)
         for j in range(nmem):
             stage[group, j, :, place] = term[j * share : (j + 1) * share]
 
@@ -121,7 +121,7 @@
         pieces = landed.at[group, pl.ds(0, nmem - 1)]
         pltpu.make_async_copy(pieces, pieces, sum_recv.at[group]).wait()
         summed = jnp.sum(landed[group].astype(jnp.float32), axis=0)
-        place = pl.ds(pl.multiple_of(group * 2 * PATCH, 2 * PATCH), 2 * PATCH)
+        place = pl.ds(pl.multiple_of(group * width, width), width)
         out_ref[:, place] = summed / jnp.float32(nmem - 1)
 
     loads[0].wait()
@@ -163,21 +163,19 @@
 
     for q in range(REACH):
         spread_patch(second, q)
-        if q % 2 == 1:
-            send_group(second * 2 + q // 2)
+        if q == REACH - 1:
+            send_group(second)
 
     for s in range(REACH):
         q = s + second * (REACH - 1 - 2 * s)
         far[s].wait_recv()
         fields[3 * REACH * first + q] = late[q]
         spread_patch(first, q)
-        if s % 2 == 1:
-            send_group(first * 2 + q // 2)
-
-    add_group(second * 2)
-    add_group(second * 2 + 1)
-    add_group(first * 2 + second)
-    add_group(first * 2 + first)
+        if s == REACH - 1:
+            send_group(first)
+
+    add_group(second)
+    add_group(first)
 
     for turn in range(2):
         pieces = held.at[turn, pl.ds(0, ncol - 1)]
@@ -185,7 +183,7 @@
     for copy in far:
         copy.wait_send()
     near.wait_send()
-    for group in range(4):
+    for group in range(2):
         pieces = stage.at[group, pl.ds(0, nmem - 1)]
         pltpu.make_async_copy(pieces, pieces, sum_send.at[group]).wait()
 
@@ -216,16 +214,16 @@
                 pltpu.VMEM((patches, slots, PATCH, PATCH), bf16),
                 pltpu.VMEM((4 * REACH + 1, levels, PATCH), bf16),
                 pltpu.VMEM((REACH, levels, PATCH), bf16),
-                pltpu.VMEM((4, nmem, share, 2 * PATCH), bf16),
-                pltpu.VMEM((4, nmem, share, 2 * PATCH), bf16),
-                dma((5,)), dma((2,)), dma((2,)), dma((REACH,)), dma((REACH,)), dma, dma, dma((4,)), dma((4,)),
+                pltpu.VMEM((2, nmem, share, REACH * PATCH), bf16),
+                pltpu.VMEM((2, nmem, share, REACH * PATCH), bf16),
+                dma((5,)), dma((2,)), dma((2,)), dma((REACH,)), dma((REACH,)), dma, dma, dma((2,)), dma((2,)),
                 pltpu.SemaphoreType.REGULAR, pltpu.SemaphoreType.REGULAR,
             ],
             compiler_params=pltpu.CompilerParams(
-                collective_id=0, has_side_effects=True, vmem_limit_bytes=60 * 1024 * 1024
+                collective_id=0, has_side_effects=True, vmem_limit_bytes=48 * 1024 * 1024
             ),
             name="localized_covariance",
-        )(members, control, vertical, blocks, neighbours, counts)
+        )(*[pltpu.with_memory_space_constraint(x, pltpu.HBM) for x in (members, control, vertical, blocks, neighbours, counts)])
 
     placed = (
         P("mem", "col", None),

time: 20.9 us -> 19.3 us (0.923)
  local copies, waits for them, and re-layouts: 1.47 us -> 0.63 us
  Pallas kernels: 19.3 us -> 18.6 us
    unnamed x1, local copies, waits for them, and re-layouts: 1.47 us -> 0.63 us
    pallas_call x1, Pallas kernels: 19.3 us -> 18.6 us  [per_device(): pl.pallas_call(functools.partial(kernel, ncol, nmem), out_shape=jax.Shape...]
where the time goes in v4:
time: 19.3 us; the launch traced here: 19.2 us
  Pallas kernels  18.6 us (96%)
  local copies, waits for them, and re-layouts  0.63 us (3%)
    pallas_call x1, Pallas kernels, per_device(): pl.pallas_call(functools.partial(kernel, ncol, nmem), out_shape=jax.Shape...  18.6 us
    unnamed x1, local copies, waits for them, and re-layouts  0.63 us

profile of v4, /device:TPU:0, one launch (start us, length us, event | category | flops | bytes accessed | tf_op | source)
XLA Modules:
  0.0 19.2 jit_solution(59933844881213194)
XLA Ops:
  0.0 18.6 %localized_covariance.1 = f32[16,1024]{1,0:T(8,128)S(1)} custom-call(bf16[1,32,4096]{2,1,0:T(8,128)(2,1)} %members.1, bf16[128,1024]{1,0:T(8,128)(2,1)} %control.1, bf16[128,128]{1,0:T(8,128)(2,1)} %vertical.1, bf16[8,8,128,128]{3,2,1,0:T(8,128)(2,1)} %blocks.1, s32[8,8]{1,0:T(8,128)} %neighbours.1, s32[8]{0:T(128)} %counts_in.1), custom_call_target="tpu_custom_call" | custom-call | tf_op jit(solution)/shard_map/localized_covariance/pallas_call | solution.py:203
  18.6 0.6 %copy.8 = f32[16,1024]{1,0:T(8,128)} copy(f32[16,1024]{1,0:T(8,128)S(1)} %localized_covariance.1) | data formatting | bytes 131072

commit v5 on v4

--- a/solution.py
+++ b/solution.py
@@ -14,7 +14,7 @@
 
 def kernel(
     ncol, nmem, members, control, vertical, blocks, neighbours, counts_in, out_ref,
-    near_ids, counts, held, ctl, vert, blk, fields, late, stage, landed,
+    slabs, near_ids, counts, held, ctl, vert, blk, fields, late, stage, landed,
     load_sem, slab_send, slab_recv, far_send, far_recv, near_send, near_recv, sum_send, sum_recv, joined, ready,
 ):
     me, mine = lax.axis_index("col"), lax.axis_index("mem")
@@ -35,6 +35,8 @@
         pltpu.make_async_copy(neighbours, near_ids, load_sem.at[3]),
         pltpu.make_async_copy(counts_in, counts, load_sem.at[4]),
     ]
+    bring = pltpu.make_async_copy(members, slabs, load_sem.at[5])
+    bring.start()
     for load in loads:
         load.start()
 
@@ -59,13 +61,15 @@
     def _():
         pl.semaphore_wait(barrier, ncol - 1)
         pl.semaphore_signal(joined, inc=1, device_id={"col": 0}, device_id_type=MESH)
+
+    bring.wait()
 
     for turn in range(2):
         for s in range(ncol):
             to = lax.rem(me + s, ncol)
             half = lax.rem(to + turn, 2)
             start = pl.multiple_of(to * columns + half * width, width)
-            source = members.at[0, :, pl.ds(start, width)]
+            source = slabs.at[0, :, pl.ds(start, width)]
             if s == 0:
                 pltpu.make_async_copy(source, held.at[half, me], slab_recv.at[half]).start()
             else:
@@ -206,6 +210,7 @@
             in_specs=[in_hbm] * 6,
             out_specs=pl.BlockSpec(memory_space=pltpu.VMEM),
             scratch_shapes=[
+                pltpu.VMEM(members.shape, bf16),
                 pltpu.SMEM((patches, slots), jnp.int32),
                 pltpu.SMEM((patches,), jnp.int32),
                 pltpu.VMEM((2, ncol, slab_rows, columns // 2), bf16),
@@ -216,7 +221,7 @@
                 pltpu.VMEM((REACH, levels, PATCH), bf16),
                 pltpu.VMEM((2, nmem, share, REACH * PATCH), bf16),
                 pltpu.VMEM((2, nmem, share, REACH * PATCH), bf16),
-                dma((5,)), dma((2,)), dma((2,)), dma((REACH,)), dma((REACH,)), dma, dma, dma((2,)), dma((2,)),
+                dma((6,)), dma((2,)), dma((2,)), dma((REACH,)), dma((REACH,)), dma, dma, dma((2,)), dma((2,)),
                 pltpu.SemaphoreType.REGULAR, pltpu.SemaphoreType.REGULAR,
             ],
             compiler_params=pltpu.CompilerParams(

time: 19.3 us -> 19.1 us (0.990)
  Pallas kernels: 18.6 us -> 18.4 us
    pallas_call x1, Pallas kernels: 18.6 us -> 18.4 us  [per_device(): pl.pallas_call(functools.partial(kernel, ncol, nmem), out_shape=jax.Shape...]
where the time goes in v5:
time: 19.1 us; the launch traced here: 19 us
  Pallas kernels  18.4 us (96%)
  local copies, waits for them, and re-layouts  0.63 us (3%)
    pallas_call x1, Pallas kernels, per_device(): pl.pallas_call(functools.partial(kernel, ncol, nmem), out_shape=jax.Shape...  18.4 us
    unnamed x1, local copies, waits for them, and re-layouts  0.63 us

profile of v5, /device:TPU:0, one launch (start us, length us, event | category | flops | bytes accessed | tf_op | source)
XLA Modules:
  0.0 19.0 jit_solution(7118285261413060906)
XLA Ops:
  0.0 18.4 %localized_covariance.1 = f32[16,1024]{1,0:T(8,128)S(1)} custom-call(bf16[1,32,4096]{2,1,0:T(8,128)(2,1)} %members.1, bf16[128,1024]{1,0:T(8,128)(2,1)} %control.1, bf16[128,128]{1,0:T(8,128)(2,1)} %vertical.1, bf16[8,8,128,128]{3,2,1,0:T(8,128)(2,1)} %blocks.1, s32[8,8]{1,0:T(8,128)} %neighbours.1, s32[8]{0:T(128)} %counts_in.1), custom_call_target="tpu_custom_call" | custom-call | tf_op jit(solution)/shard_map/localized_covariance/pallas_call | solution.py:207
  18.4 0.6 %copy.8 = f32[16,1024]{1,0:T(8,128)} copy(f32[16,1024]{1,0:T(8,128)S(1)} %localized_covariance.1) | data formatting | bytes 131072
